TPU v7x, 256 devices: a whole 4x4x8 slice. The times are simulated.
256 devices in a mesh: prow: 16 (over z, core), pcol: 16 (over x, y).
Axes of the slice: x: 4, y: 4, z: 8, core: 2. Of those that a mesh axis runs over, the one named last changes fastest.
Arguments:
- leaf_source: bfloat16 [16, 16, 8, 256, 128], P('prow', 'pcol'), may hold values from -6 to 6
- band_source: bfloat16 [16, 256, 128], P('prow'), may hold values from -6 to 6
- strip_source: bfloat16 [16, 256, 128], P('pcol'), may hold values from -6 to 6
- summit_source: bfloat16 [256, 128], replicated, may hold values from -6 to 6
- leaf_inverse: bfloat16 [16, 16, 8, 256, 256], P('prow', 'pcol'), may hold values from -1 to 2
- band_inverse: bfloat16 [16, 256, 256], P('prow'), may hold values from -1 to 2
- strip_inverse: bfloat16 [16, 256, 256], P('pcol'), may hold values from -1 to 2
- summit_inverse: bfloat16 [256, 256], replicated, may hold values from -1 to 2
- leaf_blocks: bfloat16 [16, 16, 28, 256, 256], P('prow', 'pcol'), may hold values from -0.09375 to 0.09375
- band_blocks: bfloat16 [16, 16, 8, 256, 256], P('prow', 'pcol'), may hold values from -0.0234375 to 0.0234375
- strip_blocks: bfloat16 [16, 16, 8, 256, 256], P('prow', 'pcol'), may hold values from -0.0234375 to 0.0234375
- summit_blocks: bfloat16 [16, 16, 8, 256, 256], P('prow', 'pcol'), may hold values from -0.015625 to 0.015625
- coupling: bfloat16 [16, 16, 256, 256], P('prow', 'pcol'), may hold values from -0.0625 to 0.0625
- summit_band: bfloat16 [16, 256, 256], P('prow', 'pcol'), may hold values from -0.046875 to 0.046875
- summit_strip: bfloat16 [16, 256, 256], P('pcol'), may hold values from -0.046875 to 0.046875
- parents: int32 [16, 16, 8], P('prow', 'pcol'), may hold values from 1 to 8, as said below
- widths: int32 [16, 16, 8], P('prow', 'pcol'), may hold values from 64 to 256
Outputs:
- leaf_answer: bfloat16 [16, 16, 8, 256, 128], P('prow', 'pcol')
- band_answer: bfloat16 [16, 256, 128], P('prow')
- strip_answer: bfloat16 [16, 256, 128], P('pcol')
- summit_answer: bfloat16 [256, 128], replicated
Inputs may be any that keep to these rules, and one draw needn't show every extreme that they name: parents[r, c, a] is a later leaf of the same subtree, or 8 where leaf a links only to the separators.
All inputs are finite; a program needn't handle non-finite values.
Results may differ from a plain program's by a relative error of at most 0.015.
Values sent between devices are 32-bit elements; how exact they have to be, the bound alone decides.
A program may use at most 64 MiB of HBM per device.

v0:
```python
import jax
import jax.numpy as jnp
from jax import lax
from jax.sharding import PartitionSpec as P

PASSES = 2


def ancestors(parent_list, leaf_count):
    node_ids = jnp.arange(leaf_count + 1, dtype=jnp.int32)
    current = parent_list
    extended = jnp.concatenate([current, jnp.full((1,), leaf_count, jnp.int32)])
    reached = jnp.zeros((leaf_count + 1, leaf_count), jnp.float32)
    for repeat in range(leaf_count):
        matches = current[None, :] == node_ids[:, None]
        reached = jnp.maximum(reached, matches.astype(jnp.float32))
        current = jnp.sum(jnp.where(matches, extended[:, None], 0), axis=0)
    return reached[:leaf_count]


def multiply(left, right, form):
    return jnp.einsum(form, left, right, preferred_element_type=jnp.float32)


def forward_block(inverse, source, partial_value):
    residual = (source.astype(jnp.float32) - partial_value).astype(jnp.bfloat16)
    return multiply(inverse, residual, "ij,jr->ir").astype(jnp.bfloat16)


def backward_block(inverse, source, partial_value):
    residual = (source.astype(jnp.float32) - partial_value).astype(jnp.bfloat16)
    return multiply(inverse, residual, "ji,jr->ir").astype(jnp.bfloat16)


def leaf_forward(pair_blocks, inverses, sources, reached, row_mask):
    leaf_count = sources.shape[0]
    solved = []
    for position in range(leaf_count):
        residual = sources[position].astype(jnp.float32)
        if position > 0:
            first_pair = position * (position - 1) // 2
            weights = reached[position, :position].astype(jnp.bfloat16)
            stacked = jnp.stack(solved) * weights[:, None, None]
            residual = residual - multiply(
                pair_blocks[first_pair : first_pair + position], stacked, "bij,bjr->ir"
            )
        residual = (row_mask[position] * residual).astype(jnp.bfloat16)
        solved.append(
            (row_mask[position] * multiply(inverses[position], residual, "ij,jr->ir")).astype(
                jnp.bfloat16
            )
        )
    return jnp.stack(solved)


def leaf_backward(pair_blocks, inverses, solved, outer, reached, row_mask):
    leaf_count = solved.shape[0]
    pending = outer
    answers = [None] * leaf_count
    for position in reversed(range(leaf_count)):
        residual = (
            row_mask[position] * (solved[position].astype(jnp.float32) - pending[position])
        ).astype(jnp.bfloat16)
        update = (row_mask[position] * multiply(inverses[position], residual, "ji,jr->ir")).astype(
            jnp.bfloat16
        )
        answers[position] = update
        if position > 0:
            first_pair = position * (position - 1) // 2
            pushed = multiply(
                pair_blocks[first_pair : first_pair + position], update, "bji,jr->bir"
            )
            pending = pending.at[:position].add(
                reached[position, :position][:, None, None] * pushed
            )
    return jnp.stack(answers)


def per_device(
    leaf_source,
    band_source,
    strip_source,
    summit_source,
    leaf_inverse,
    band_inverse,
    strip_inverse,
    summit_inverse,
    leaf_blocks,
    band_blocks,
    strip_blocks,
    summit_blocks,
    coupling,
    summit_band,
    summit_strip,
    parents,
    widths,
):
    leaf_count = leaf_source.shape[2]
    block_width = leaf_source.shape[3]
    reached = ancestors(parents[0, 0], leaf_count)
    column_ids = jnp.arange(block_width, dtype=jnp.int32)
    row_mask = (column_ids[None, :] < widths[0, 0][:, None]).astype(jnp.float32)[:, :, None]
    band_slab = summit_band.shape[1]
    strip_slab = block_width // lax.axis_size("prow")
    column_place = lax.axis_index("pcol") * band_slab
    row_place = lax.axis_index("prow") * strip_slab
    inverses = leaf_inverse[0, 0]
    pair_blocks = leaf_blocks[0, 0]
    to_band = band_blocks[0, 0]
    to_strip = strip_blocks[0, 0]
    to_summit = summit_blocks[0, 0]
    link_block = coupling[0, 0]
    lift_band = summit_band[0]
    lift_strip = summit_strip[0]
    current = (leaf_source[0, 0], band_source[0], strip_source[0], summit_source)
    for iteration in range(PASSES):
        leaf_now, band_now, strip_now, summit_now = current
        solved = leaf_forward(pair_blocks, inverses, leaf_now, reached, row_mask)
        band_term = multiply(to_band, solved, "aij,ajr->ir")
        strip_term = multiply(to_strip, solved, "aij,ajr->ir")
        summit_term = multiply(to_summit, solved, "aij,ajr->ir")
        band_partial = lax.psum(band_term, "pcol")
        band_solved = forward_block(band_inverse[0], band_now, band_partial)
        own_band = lax.dynamic_slice_in_dim(band_solved, column_place, band_slab, 0)
        summit_term = summit_term + multiply(lift_band, own_band, "ki,kn->in")
        strip_term = strip_term + multiply(link_block, band_solved, "ij,jn->in")
        strip_partial = lax.psum(strip_term, "prow")
        strip_solved = forward_block(strip_inverse[0], strip_now, strip_partial)
        own_lift = lax.dynamic_slice_in_dim(lift_strip, row_place, strip_slab, 0)
        own_strip = lax.dynamic_slice_in_dim(strip_solved, row_place, strip_slab, 0)
        summit_partial = lax.psum(
            summit_term + multiply(own_lift, own_strip, "ki,kn->in"), ("prow", "pcol")
        )
        summit_solved = forward_block(summit_inverse, summit_now, summit_partial)
        summit_answer = backward_block(
            summit_inverse, summit_solved, jnp.zeros(summit_solved.shape, jnp.float32)
        )
        strip_answer = backward_block(
            strip_inverse[0], strip_solved, multiply(lift_strip, summit_answer, "ki,in->kn")
        )
        downward = multiply(link_block, strip_answer, "ji,jn->in")
        band_piece = multiply(lift_band, summit_answer, "ki,in->kn")
        band_back = lax.psum(downward, "pcol") + lax.all_gather(
            band_piece, "pcol", axis=0, tiled=True
        )
        band_answer = backward_block(band_inverse[0], band_solved, band_back)
        outer = (
            multiply(to_band, band_answer, "aij,ir->ajr")
            + multiply(to_strip, strip_answer, "aij,ir->ajr")
            + multiply(to_summit, summit_answer, "aij,ir->ajr")
        )
        leaf_answer = leaf_backward(pair_blocks, inverses, solved, outer, reached, row_mask)
        current = (leaf_answer, band_answer, strip_answer, summit_answer)
    return (current[0][None, None], current[1][None], current[2][None], current[3])


def solution(mesh):
    placed = (
        P("prow", "pcol", None, None, None),
        P("prow", None, None),
        P("pcol", None, None),
        P(),
        P("prow", "pcol", None, None, None),
        P("prow", None, None),
        P("pcol", None, None),
        P(),
        P("prow", "pcol", None, None, None),
        P("prow", "pcol", None, None, None),
        P("prow", "pcol", None, None, None),
        P("prow", "pcol", None, None, None),
        P("prow", "pcol", None, None),
        P("prow", "pcol", None),
        P("pcol", None, None),
        P("prow", "pcol", None),
        P("prow", "pcol", None),
    )
    return jax.shard_map(
        per_device,
        mesh=mesh,
        in_specs=placed,
        out_specs=(
            P("prow", "pcol", None, None, None),
            P("prow", None, None),
            P("pcol", None, None),
            P(),
        ),
        check_vma=False,
    )
```

profile of v0, /device:TPU:2, one launch (start us, length us, event | category | flops | bytes accessed | tf_op | source)
XLA Modules:
  0.0 1181.8 jit_solution(3843605746356094015)
XLA Ops:
  22.1 2.2 constant_dynamic-update-slice_fusion.13
  25.3 2.5 constant_dynamic-update-slice_fusion.12
  28.6 2.6 constant_dynamic-update-slice_fusion.11
  31.2 2.6 constant_dynamic-update-slice_fusion.18
  33.8 2.2 convolution_bitcast_fusion.19
  46.5 84.6 %all-reduce.9.cloned.1.call-done = f32[256,128]{1,0:T(8,128)} async-done(((f32[256,128]{1,0:T(8,128)}), f32[256,128]{1,0:T(8,128)}) %all-reduce.9.cloned.1.call-update) | async-done | bytes 131088 | tf_op jit(solution)/shard_map/psum | solution.py:122
  136.7 105.3 %all-reduce.11.cloned.1.call-done = f32[256,128]{1,0:T(8,128)} async-done(((f32[256,128]{1,0:T(8,128)}), f32[256,128]{1,0:T(8,128)}) %all-reduce.11.cloned.1.call-update) | async-done | bytes 131088 | tf_op jit(solution)/shard_map/psum | solution.py:127
  246.8 243.6 %all-reduce.13.cloned.1.call-done = f32[256,128]{1,0:T(8,128)} async-done(((f32[256,128]{1,0:T(8,128)}), f32[256,128]{1,0:T(8,128)}) %all-reduce.13.cloned.1.call-update) | async-done | bytes 131088 | tf_op jit(solution)/shard_map/psum | solution.py:131
  496.9 23.8 %all_gather.6 = f32[256,128]{1,0:T(8,128)} all-gather(f32[16,128]{1,0:T(8,128)S(1)} %convolution_bitcast_fusion.22), channel_id=1, replica_groups=mesh['prow'=16,'pcol'=16] {'pcol'}, dimensions={0}, use_global_device_ids=true | all-gather | bytes 139264 | tf_op jit(solution)/shard_map/all_gather | solution.py:143
  522.3 62.3 %all-reduce.15.cloned.1.call-done = f32[256,128]{0,1:T(8,128)} async-done(((f32[256,128]{0,1:T(8,128)}), f32[256,128]{0,1:T(8,128)}) %all-reduce.15.cloned.1.call-update) | async-done | bytes 131088 | tf_op jit(solution)/shard_map/psum | solution.py:143
  599.0 2.2 constant_dynamic-update-slice_fusion.41
  601.2 2.4 constant_dynamic-update-slice_fusion.40
  603.6 2.4 constant_dynamic-update-slice_fusion.39
  606.0 2.5 constant_dynamic-update-slice_fusion.38
  608.5 2.6 constant_dynamic-update-slice_fusion.37
  611.1 2.7 constant_dynamic-update-slice_fusion.44
  613.8 2.2 convolution_bitcast_fusion.13
  616.0 2.2 convolution_bitcast_fusion.15
  618.2 2.2 convolution_bitcast_fusion.14
  620.4 89.7 %all-reduce.17.cloned.1.call-done = f32[256,128]{0,1:T(8,128)} async-done(((f32[256,128]{0,1:T(8,128)}), f32[256,128]{0,1:T(8,128)}) %all-reduce.17.cloned.1.call-update) | async-done | bytes 131088 | tf_op jit(solution)/shard_map/psum | solution.py:122
  715.6 105.4 %all-reduce.19.cloned.1.call-done = f32[256,128]{0,1:T(8,128)} async-done(((f32[256,128]{0,1:T(8,128)}), f32[256,128]{0,1:T(8,128)}) %all-reduce.19.cloned.1.call-update) | async-done | bytes 131088 | tf_op jit(solution)/shard_map/psum | solution.py:127
  824.6 245.8 %all-reduce.21.cloned.1.call-done = f32[256,128]{0,1:T(8,128)} async-done(((f32[256,128]{0,1:T(8,128)}), f32[256,128]{0,1:T(8,128)}) %all-reduce.21.cloned.1.call-update) | async-done | bytes 131088 | tf_op jit(solution)/shard_map/psum | solution.py:131
  1077.7 22.2 %all_gather.7 = f32[256,128]{1,0:T(8,128)S(1)} all-gather(f32[16,128]{1,0:T(8,128)S(1)} %convolution_bitcast_fusion.21), channel_id=1, replica_groups=mesh['prow'=16,'pcol'=16] {'pcol'}, dimensions={0}, use_global_device_ids=true | all-gather | bytes 139264 | tf_op jit(solution)/shard_map/all_gather | solution.py:143
  1100.7 62.5 %all-reduce.23.cloned.1.call-done = f32[256,128]{0,1:T(8,128)} async-done(((f32[256,128]{0,1:T(8,128)}), f32[256,128]{0,1:T(8,128)}) %all-reduce.23.cloned.1.call-update) | async-done | bytes 131088 | tf_op jit(solution)/shard_map/psum | solution.py:143
  (293 shorter events, 86.9 us)
Async XLA Ops:
  7.2 26.6 %copy-start = (bf16[1,1,8,256,256]{4,3,2,1,0:T(8,128)(2,1)S(1)}, bf16[1,1,8,256,256]{4,3,2,1,0:T(8,128)(2,1)}, u32[]{:S(2)}) copy-start(bf16[1,1,8,256,256]{4,3,2,1,0:T(8,128)(2,1)} %param.54) | copy-start | bytes 3145732
  7.2 124.0 %all-reduce.9.cloned.1.call-start = ((), (), s32[]{:S(2)}) async-start(), calls=%async_computation | async-start | bytes 262144 | tf_op jit(solution)/shard_map/psum | solution.py:122
  10.6 20.6 %copy-start.79 = (bf16[7]{0:T(256)(128)(2,1)}, bf16[7]{0:T(256)(128)(2,1)S(1)}, u32[]{:S(2)}) copy-start(bf16[7]{0:T(256)(128)(2,1)S(1)} %fusion.590) | copy-start | bytes 46
  10.6 18.0 %copy-start.80 = (bf16[6]{0:T(256)(128)(2,1)}, bf16[6]{0:T(256)(128)(2,1)S(1)}, u32[]{:S(2)}) copy-start(bf16[6]{0:T(256)(128)(2,1)S(1)} %fusion.589) | copy-start | bytes 40
  10.6 14.7 %copy-start.81 = (bf16[5]{0:T(256)(128)(2,1)}, bf16[5]{0:T(256)(128)(2,1)S(1)}, u32[]{:S(2)}) copy-start(bf16[5]{0:T(256)(128)(2,1)S(1)} %fusion.588) | copy-start | bytes 34
  10.7 13.6 %copy-start.82 = (bf16[4]{0:T(256)(128)(2,1)}, bf16[4]{0:T(256)(128)(2,1)S(1)}, u32[]{:S(2)}) copy-start(bf16[4]{0:T(256)(128)(2,1)S(1)} %fusion.587) | copy-start | bytes 28
  10.7 13.6 %copy-start.83 = (bf16[3]{0:T(256)(128)(2,1)}, bf16[3]{0:T(256)(128)(2,1)S(1)}, u32[]{:S(2)}) copy-start(bf16[3]{0:T(256)(128)(2,1)S(1)} %fusion.586) | copy-start | bytes 22
  10.7 13.6 %copy-start.84 = (bf16[2]{0:T(256)(128)(2,1)}, bf16[2]{0:T(256)(128)(2,1)S(1)}, u32[]{:S(2)}) copy-start(bf16[2]{0:T(256)(128)(2,1)S(1)} %fusion.585) | copy-start | bytes 16
  12.2 16.4 %copy-start.54 = (f32[1,256]{1,0:T(1,128)}, f32[1,256]{1,0:T(1,128)S(1)}, u32[]{:S(2)}) copy-start(f32[1,256]{1,0:T(1,128)S(1)} %get-tuple-element.238) | copy-start | bytes 3076
  12.2 19.0 %copy-start.57 = (f32[1,256]{1,0:T(1,128)}, f32[1,256]{1,0:T(1,128)S(1)}, u32[]{:S(2)}) copy-start(f32[1,256]{1,0:T(1,128)S(1)} %get-tuple-element.237) | copy-start | bytes 3076
  25.3 17.0 %copy-start.2 = (bf16[1,1,8,256,256]{4,3,2,1,0:T(8,128)(2,1)S(1)}, bf16[1,1,8,256,256]{4,3,2,1,0:T(8,128)(2,1)}, u32[]{:S(2)}) copy-start(bf16[1,1,8,256,256]{4,3,2,1,0:T(8,128)(2,1)} %param.56) | copy-start | bytes 3145732
  28.6 15.8 %copy-start.1 = (bf16[1,1,8,256,256]{4,3,2,1,0:T(8,128)(2,1)S(1)}, bf16[1,1,8,256,256]{4,3,2,1,0:T(8,128)(2,1)}, u32[]{:S(2)}) copy-start(bf16[1,1,8,256,256]{4,3,2,1,0:T(8,128)(2,1)} %param.55) | copy-start | bytes 3145732
  31.2 101.8 %copy-start.9 = (bf16[1,1,256,256]{3,2,1,0:T(8,128)(2,1)S(1)}, bf16[1,1,256,256]{3,2,1,0:T(8,128)(2,1)}, u32[]{:S(2)}) copy-start(bf16[1,1,256,256]{3,2,1,0:T(8,128)(2,1)} %param.57) | copy-start | bytes 393220
  33.8 101.0 %copy-start.25 = (bf16[1,16,256]{2,1,0:T(8,128)(2,1)S(1)}, bf16[1,16,256]{2,1,0:T(8,128)(2,1)}, u32[]{:S(2)}) copy-start(bf16[1,16,256]{2,1,0:T(8,128)(2,1)} %param.58) | copy-start | bytes 24580
  33.8 208.2 %copy-start.8 = (bf16[1,256,256]{2,1,0:T(8,128)(2,1)S(1)}, bf16[1,256,256]{2,1,0:T(8,128)(2,1)}, u32[]{:S(2)}) copy-start(bf16[1,256,256]{2,1,0:T(8,128)(2,1)} %param.51) | copy-start | bytes 393220
  33.8 456.7 %copy-start.10 = (bf16[256,256]{1,0:T(8,128)(2,1)S(1)}, bf16[256,256]{1,0:T(8,128)(2,1)}, u32[]{:S(2)}) copy-start(bf16[256,256]{1,0:T(8,128)(2,1)} %param.52) | copy-start | bytes 393220
  36.0 206.0 %all-reduce.11.cloned.1.call-start = ((), (), s32[]{:S(2)}) async-start(), calls=%async_computation.1 | async-start | bytes 262144 | tf_op jit(solution)/shard_map/psum | solution.py:127
  134.8 355.7 %all-reduce.13.cloned.1.call-start = ((), (), s32[]{:S(2)}) async-start(), calls=%async_computation.2 | async-start | bytes 262144 | tf_op jit(solution)/shard_map/psum | solution.py:131
  245.6 339.0 %all-reduce.15.cloned.1.call-start = ((), (), s32[]{:S(2)}) async-start(), calls=%async_computation.3 | async-start | bytes 262144 | tf_op jit(solution)/shard_map/psum | solution.py:143
  495.9 214.2 %all-reduce.17.cloned.1.call-start = ((), (), s32[]{:S(2)}) async-start(), calls=%async_computation.4 | async-start | bytes 262144 | tf_op jit(solution)/shard_map/psum | solution.py:122
  618.2 202.9 %all-reduce.19.cloned.1.call-start = ((), (), s32[]{:S(2)}) async-start(), calls=%async_computation.5 | async-start | bytes 262144 | tf_op jit(solution)/shard_map/psum | solution.py:127
  713.8 356.7 %all-reduce.21.cloned.1.call-start = ((), (), s32[]{:S(2)}) async-start(), calls=%async_computation.6 | async-start | bytes 262144 | tf_op jit(solution)/shard_map/psum | solution.py:131
  824.6 338.6 %all-reduce.23.cloned.1.call-start = ((), (), s32[]{:S(2)}) async-start(), calls=%async_computation.7 | async-start | bytes 262144 | tf_op jit(solution)/shard_map/psum | solution.py:143
  1073.5 94.6 %copy-start.11 = (bf16[128,256]{1,0:T(8,128)(2,1)S(1)}, bf16[128,256]{1,0:T(8,128)(2,1)}, u32[]{:S(2)}) copy-start(bf16[128,256]{1,0:T(8,128)(2,1)} %convolution_convert_fusion.2) | copy-start | bytes 196612
  (69 other events, 185.5 us)
Sparse Core Ops, SparseCore 0:
  36.1 94.9 all-reduce.8
  134.9 107.0 all-reduce.10
  248.1 242.3 all-reduce.12
  496.0 88.5 all-reduce.14
  618.3 91.8 all-reduce.16
  713.9 107.1 all-reduce.18
  828.0 242.3 all-reduce.20
  1074.5 88.5 all-reduce.22
where the time goes:
time: 1180 us
  waiting for transfers between devices  999 us (85%)
  matrix products  92.7 us (8%)
  blocking collectives  46 us (4%)
  local copies, waits for them, and re-layouts  23.6 us (2%)
  between operations  16.2 us (1%)
    psum x2, waiting for transfers between devices, per_device(): lax.psum(summit_term + multiply(own_lift, own_strip, 'ki,kn->in'), ('prow...  489 us
    psum x2, waiting for transfers between devices, per_device(): strip_partial = lax.psum(strip_term, 'prow')  211 us
    psum x2, waiting for transfers between devices, per_device(): band_partial = lax.psum(band_term, 'pcol')  174 us
    psum x2, waiting for transfers between devices, per_device(): lax.psum(downward, 'pcol')  125 us
    dot_general x76, matrix products, multiply(): return jnp.einsum(form, left, right, preferred_element_type=jnp.float32)  92.7 us
    all_gather x2, blocking collectives, per_device(): lax.all_gather(band_piece, 'pcol', axis=0, tiled=True)  46 us
  transfers between devices with their start and end apart: 8, of which 8 were waited for; matrix products, arithmetic and copies ran while one was open for 2% of the time, Pallas kernels for 0%

commit v1 on v0

--- a/solution.py
+++ b/solution.py
@@ -4,6 +4,18 @@
 from jax.sharding import PartitionSpec as P
 
 PASSES = 2
+
+
+def tracks_place(payload, dev_axis):
+    x_now, arr_next = (payload, 0)
+    n_peers_all = lax.axis_size(dev_axis)
+    while 1 << arr_next < n_peers_all:
+        w2 = map(lambda pp: (pp, pp ^ 1 << arr_next), range(n_peers_all))
+        part_now = list(w2)
+        o_now = lax.ppermute(x_now, axis_name=dev_axis, perm=part_now)
+        x_now = x_now + o_now
+        arr_next = arr_next + 1
+    return x_now
 
 
 def ancestors(parent_list, leaf_count):
@@ -119,7 +131,7 @@
         band_term = multiply(to_band, solved, "aij,ajr->ir")
         strip_term = multiply(to_strip, solved, "aij,ajr->ir")
         summit_term = multiply(to_summit, solved, "aij,ajr->ir")
-        band_partial = lax.psum(band_term, "pcol")
+        band_partial = tracks_place(band_term, "pcol")
         band_solved = forward_block(band_inverse[0], band_now, band_partial)
         own_band = lax.dynamic_slice_in_dim(band_solved, column_place, band_slab, 0)
         summit_term = summit_term + multiply(lift_band, own_band, "ki,kn->in")

time: 1180 us -> 1040 us (0.88)
  waiting for transfers between devices: 999 us -> 853 us
  starting transfers between devices: 0.33 us -> 12.5 us
    psum x2 -> x0, waiting for transfers between devices: 174 us -> none  [per_device(): band_partial = lax.psum(band_term, 'pcol')]
    ppermute x0 -> x8, waiting for transfers between devices: none -> 24.7 us  [tracks_place(): o_now = lax.ppermute(x_now, axis_name=dev_axis, perm=part_now)]
    ppermute x0 -> x8, starting transfers between devices: none -> 12.2 us  [tracks_place(): o_now = lax.ppermute(x_now, axis_name=dev_axis, perm=part_now)]
  transfers between devices with their start and end apart: 8 -> 14, of which waited for: 8 -> 13; matrix products, arithmetic and copies ran while one was open for 2% -> 2% of each run, Pallas kernels for 0% -> 0%
where the time goes in v1:
time: 1040 us
  waiting for transfers between devices  853 us (82%)
  matrix products  85.8 us (8%)
  blocking collectives  46.2 us (4%)
  local copies, waits for them, and re-layouts  23.3 us (2%)
  between operations  16.2 us (2%)
  starting transfers between devices  12.5 us (1%)
    psum x2, waiting for transfers between devices, per_device(): lax.psum(summit_term + multiply(own_lift, own_strip, 'ki,kn->in'), ('prow...  490 us
    psum x2, waiting for transfers between devices, per_device(): strip_partial = lax.psum(strip_term, 'prow')  214 us
    psum x2, waiting for transfers between devices, per_device(): lax.psum(downward, 'pcol')  125 us
    dot_general x76, matrix products, multiply(): return jnp.einsum(form, left, right, preferred_element_type=jnp.float32)  85.8 us
    all_gather x2, blocking collectives, per_device(): lax.all_gather(band_piece, 'pcol', axis=0, tiled=True)  46.2 us
    ppermute x8, waiting for transfers between devices, tracks_place(): o_now = lax.ppermute(x_now, axis_name=dev_axis, perm=part_now)  24.7 us
  transfers between devices with their start and end apart: 14, of which 13 were waited for; matrix products, arithmetic and copies ran while one was open for 2% of the time, Pallas kernels for 0%

profile of v1, /device:TPU:2, one launch (start us, length us, event | category | flops | bytes accessed | tf_op | source)
XLA Modules:
  0.0 1042.0 jit_solution(14149702212234950948)
XLA Ops:
  22.1 2.2 constant_dynamic-update-slice_fusion.13
  24.5 2.3 constant_dynamic-update-slice_fusion.12
  26.8 2.6 constant_dynamic-update-slice_fusion.11
  29.4 2.7 constant_dynamic-update-slice_fusion.18
  43.3 3.0 collective-permute-start.1
  47.5 2.3 collective-permute-done.1
  55.0 3.0 collective-permute-start.3
  65.1 108.8 %all-reduce.7.cloned.1.call-done = f32[256,128]{1,0:T(8,128)} async-done(((f32[256,128]{1,0:T(8,128)}), f32[256,128]{1,0:T(8,128)}) %all-reduce.7.cloned.1.call-update) | async-done | bytes 131088 | tf_op jit(solution)/shard_map/psum | solution.py:139
  178.7 244.6 %all-reduce.9.cloned.1.call-done = f32[256,128]{1,0:T(8,128)} async-done(((f32[256,128]{1,0:T(8,128)}), f32[256,128]{1,0:T(8,128)}) %all-reduce.9.cloned.1.call-update) | async-done | bytes 131088 | tf_op jit(solution)/shard_map/psum | solution.py:143
  429.7 23.9 %all_gather.6 = f32[256,128]{1,0:T(8,128)} all-gather(f32[16,128]{1,0:T(8,128)S(1)} %convolution_bitcast_fusion.22), channel_id=1, replica_groups=mesh['prow'=16,'pcol'=16] {'pcol'}, dimensions={0}, use_global_device_ids=true | all-gather | bytes 139264 | tf_op jit(solution)/shard_map/all_gather | solution.py:155
  455.3 62.2 %all-reduce.11.cloned.1.call-done = f32[256,128]{0,1:T(8,128)} async-done(((f32[256,128]{0,1:T(8,128)}), f32[256,128]{0,1:T(8,128)}) %all-reduce.11.cloned.1.call-update) | async-done | bytes 131088 | tf_op jit(solution)/shard_map/psum | solution.py:155
  533.9 2.4 constant_dynamic-update-slice_fusion.40
  536.3 2.4 constant_dynamic-update-slice_fusion.39
  538.7 2.5 constant_dynamic-update-slice_fusion.38
  541.2 2.6 constant_dynamic-update-slice_fusion.37
  543.8 2.7 constant_dynamic-update-slice_fusion.44
  548.5 4.8 collective-permute-done.4
  554.8 5.1 collective-permute-done.5
  562.9 3.4 collective-permute-done.6
  568.0 4.8 collective-permute-done.7
  576.4 105.1 %all-reduce.13.cloned.1.call-done = f32[256,128]{0,1:T(8,128)} async-done(((f32[256,128]{0,1:T(8,128)}), f32[256,128]{0,1:T(8,128)}) %all-reduce.13.cloned.1.call-update) | async-done | bytes 131088 | tf_op jit(solution)/shard_map/psum | solution.py:139
  685.1 245.6 %all-reduce.15.cloned.1.call-done = f32[256,128]{0,1:T(8,128)} async-done(((f32[256,128]{0,1:T(8,128)}), f32[256,128]{0,1:T(8,128)}) %all-reduce.15.cloned.1.call-update) | async-done | bytes 131088 | tf_op jit(solution)/shard_map/psum | solution.py:143
  938.0 22.3 %all_gather.7 = f32[256,128]{1,0:T(8,128)S(1)} all-gather(f32[16,128]{1,0:T(8,128)S(1)} %convolution_bitcast_fusion.21), channel_id=1, replica_groups=mesh['prow'=16,'pcol'=16] {'pcol'}, dimensions={0}, use_global_device_ids=true | all-gather | bytes 139264 | tf_op jit(solution)/shard_map/all_gather | solution.py:155
  961.0 62.4 %all-reduce.17.cloned.1.call-done = f32[256,128]{0,1:T(8,128)} async-done(((f32[256,128]{0,1:T(8,128)}), f32[256,128]{0,1:T(8,128)}) %all-reduce.17.cloned.1.call-update) | async-done | bytes 131088 | tf_op jit(solution)/shard_map/psum | solution.py:155
  (316 shorter events, 102.2 us)
Async XLA Ops:
  7.2 24.9 %copy-start = (bf16[1,1,8,256,256]{4,3,2,1,0:T(8,128)(2,1)S(1)}, bf16[1,1,8,256,256]{4,3,2,1,0:T(8,128)(2,1)}, u32[]{:S(2)}) copy-start(bf16[1,1,8,256,256]{4,3,2,1,0:T(8,128)(2,1)} %param.54) | copy-start | bytes 3145732
  7.2 166.7 %all-reduce.7.cloned.1.call-start = ((), (), s32[]{:S(2)}) async-start(), calls=%async_computation | async-start | bytes 262144 | tf_op jit(solution)/shard_map/psum | solution.py:139
  26.8 23.9 %copy-start.2 = (bf16[1,1,8,256,256]{4,3,2,1,0:T(8,128)(2,1)S(1)}, bf16[1,1,8,256,256]{4,3,2,1,0:T(8,128)(2,1)}, u32[]{:S(2)}) copy-start(bf16[1,1,8,256,256]{4,3,2,1,0:T(8,128)(2,1)} %param.56) | copy-start | bytes 3145732
  29.4 28.6 %copy-start.1 = (bf16[1,1,8,256,256]{4,3,2,1,0:T(8,128)(2,1)S(1)}, bf16[1,1,8,256,256]{4,3,2,1,0:T(8,128)(2,1)}, u32[]{:S(2)}) copy-start(bf16[1,1,8,256,256]{4,3,2,1,0:T(8,128)(2,1)} %param.55) | copy-start | bytes 3145732
  32.1 30.3 %copy-start.10 = (bf16[1,1,256,256]{3,2,1,0:T(8,128)(2,1)S(1)}, bf16[1,1,256,256]{3,2,1,0:T(8,128)(2,1)}, u32[]{:S(2)}) copy-start(bf16[1,1,256,256]{3,2,1,0:T(8,128)(2,1)} %param.57) | copy-start | bytes 393220
  32.1 31.2 %copy-start.30 = (bf16[1,16,256]{2,1,0:T(8,128)(2,1)S(1)}, bf16[1,16,256]{2,1,0:T(8,128)(2,1)}, u32[]{:S(2)}) copy-start(bf16[1,16,256]{2,1,0:T(8,128)(2,1)} %param.58) | copy-start | bytes 24580
  32.1 141.8 %copy-start.9 = (bf16[1,256,256]{2,1,0:T(8,128)(2,1)S(1)}, bf16[1,256,256]{2,1,0:T(8,128)(2,1)}, u32[]{:S(2)}) copy-start(bf16[1,256,256]{2,1,0:T(8,128)(2,1)} %param.51) | copy-start | bytes 393220
  34.3 389.0 %copy-start.11 = (bf16[256,256]{1,0:T(8,128)(2,1)S(1)}, bf16[256,256]{1,0:T(8,128)(2,1)}, u32[]{:S(2)}) copy-start(bf16[256,256]{1,0:T(8,128)(2,1)} %param.52) | copy-start | bytes 393220
  34.3 8.0 collective-permute-start
  43.3 6.6 collective-permute-start.1
  49.9 5.1 collective-permute-start.2
  55.0 6.6 collective-permute-start.3
  63.2 360.1 %all-reduce.9.cloned.1.call-start = ((), (), s32[]{:S(2)}) async-start(), calls=%async_computation.1 | async-start | bytes 262144 | tf_op jit(solution)/shard_map/psum | solution.py:143
  177.5 340.0 %all-reduce.11.cloned.1.call-start = ((), (), s32[]{:S(2)}) async-start(), calls=%async_computation.2 | async-start | bytes 262144 | tf_op jit(solution)/shard_map/psum | solution.py:155
  428.7 252.8 %all-reduce.13.cloned.1.call-start = ((), (), s32[]{:S(2)}) async-start(), calls=%async_computation.3 | async-start | bytes 262144 | tf_op jit(solution)/shard_map/psum | solution.py:139
  546.5 26.3 %copy-start.13 = (bf16[1,256,256]{2,1,0:T(8,128)(2,1)S(1)}, bf16[1,256,256]{2,1,0:T(8,128)(2,1)}, u32[]{:S(2)}) copy-start(bf16[1,256,256]{2,1,0:T(8,128)(2,1)} %param.50) | copy-start | bytes 393220
  546.5 26.3 %copy-start.19 = (bf16[128,256]{1,0:T(8,128)(2,1)S(1)}, bf16[128,256]{1,0:T(8,128)(2,1)}, u32[]{:S(2)}) copy-start(bf16[128,256]{1,0:T(8,128)(2,1)} %copy-done.18) | copy-start | bytes 196612
  548.1 5.2 collective-permute-start.4
  553.3 6.6 collective-permute-start.5
  559.9 6.3 collective-permute-start.6
  566.3 6.6 collective-permute-start.7
  574.5 356.2 %all-reduce.15.cloned.1.call-start = ((), (), s32[]{:S(2)}) async-start(), calls=%async_computation.4 | async-start | bytes 262144 | tf_op jit(solution)/shard_map/psum | solution.py:143
  685.1 338.4 %all-reduce.17.cloned.1.call-start = ((), (), s32[]{:S(2)}) async-start(), calls=%async_computation.5 | async-start | bytes 262144 | tf_op jit(solution)/shard_map/psum | solution.py:155
  933.9 94.5 %copy-start.14 = (bf16[128,256]{1,0:T(8,128)(2,1)S(1)}, bf16[128,256]{1,0:T(8,128)(2,1)}, u32[]{:S(2)}) copy-start(bf16[128,256]{1,0:T(8,128)(2,1)} %convolution_convert_fusion.2) | copy-start | bytes 196612
  (78 other events, 365.5 us)
Sparse Core Ops, SparseCore 0:
  63.3 110.5 all-reduce.6
  180.9 242.3 all-reduce.8
  428.8 88.5 all-reduce.10
  574.6 106.8 all-reduce.12
  688.3 242.3 all-reduce.14
  934.8 88.5 all-reduce.16
